TPU v7x, 512 devices: a whole 4x8x8 slice. The times are simulated.
512 devices in a mesh: lat: 64 (over x, y, z_lo), lev: 8 (over z_hi, core).
Axes of the slice: x: 4, y: 8, z: 8 (z_hi: 4, z_lo: 2; z = z_hi * 2 + z_lo), core: 2. Of those that a mesh axis runs over, the one named last changes fastest.
Arguments:
- winds: float32 [2, 16, 256, 1152], P(None, 'lev', 'lat'), may hold values from -5 to 5
- fields: float32 [5, 16, 256, 1152], P(None, 'lev', 'lat'), may hold values from -6 to 6
- thickness: float32 [16, 256, 1152], P('lev', 'lat'), may hold values from 0.5 to 2
- filter_mask: int32 [256], P('lat'), may hold values from 0 to 1
- cutoff: int32 [256], P('lat'), may hold values from 1 to 576
Outputs:
- winds_out: float32 [2, 16, 256, 1152], P(None, 'lev', 'lat')
- fields_out: float32 [5, 16, 256, 1152], P(None, 'lev', 'lat')
- column_mass: float32 [256, 1152], P('lat', 'lev')
All inputs are finite; a program needn't handle non-finite values.
Results may differ from a plain program's by a relative error of at most 0.0003.
Values sent between devices are 32-bit elements; how exact they have to be, the bound alone decides.
No kernel may reach another device: no remote copies, remote signals or barrier semaphores. Data moves between devices by JAX's collectives and lax.ppermute only.
A program may use at most 64 MiB of HBM per device.

v0:
```python
import math

import jax
import jax.numpy as jnp
import numpy as np
from jax import lax
from jax.experimental import pallas as pl
from jax.experimental.pallas import tpu as pltpu
from jax.sharding import PartitionSpec as P

NSUB = 2
COEF = 0.08
LANES = 128
RADIX = 9
LON = RADIX * LANES
HALF = RADIX // 2 + 1
ROWS = 4
TILES = 16
EXTRA = 16


def make_tables():
    n2 = np.arange(LANES)
    k1 = np.arange(HALF)
    theta = 2.0 * math.pi * k1[:, None] * n2[None, :] / LON
    k = k1[:, None] + RADIX * n2[None, :]
    k = np.minimum(k, LON - k)
    inverse = np.where(k > 0, 1.0 / np.maximum(k, 1) ** 2, 0.0)
    scale = np.where(k > 0, np.where(k1[:, None] == 0, 1.0, 2.0) / LON, 0.0)
    table = np.zeros((4, 8, LANES), np.float32)
    table[0, :HALF] = np.cos(theta)
    table[1, :HALF] = np.sin(theta)
    table[2, :HALF] = inverse
    table[3, :HALF] = scale
    angle = 2.0 * math.pi * (n2[:, None] * n2[None, :] % LANES) / LANES
    cosine, sine = np.cos(angle), np.sin(angle)
    dense = np.block([[cosine, -sine], [sine, cosine]]).astype(np.float32)
    high = dense.astype(jnp.bfloat16)
    low = (dense - high.astype(np.float32)).astype(jnp.bfloat16)
    return table, high, low


def split_dot(left, high, low):
    left_high = left.astype(jnp.bfloat16)
    left_low = (left - left_high.astype(jnp.float32)).astype(jnp.bfloat16)
    dot = lambda a, b: jnp.dot(a, b, preferred_element_type=jnp.float32)
    return dot(left_high, high) + (dot(left_low, high) + dot(left_high, low))


def polar_filter(rows, wind_ref, square_ref, keep_ref, table_ref, high_ref, low_ref):
    blocks = [wind_ref[:rows, LANES * j : LANES * (j + 1)] for j in range(RADIX)]
    plus = [blocks[j] + blocks[RADIX - j] for j in range(1, HALF)]
    minus = [blocks[j] - blocks[RADIX - j] for j in range(1, HALF)]
    cosine = lambda a: math.cos(2.0 * math.pi * (a % RADIX) / RADIX)
    sine = lambda a: math.sin(2.0 * math.pi * (a % RADIX) / RADIX)
    real, imag = [blocks[0] + ((plus[0] + plus[1]) + (plus[2] + plus[3]))], [jnp.zeros_like(blocks[0])]
    for k in range(1, HALF):
        re = blocks[0]
        im = None
        for j in range(1, HALF):
            re = re + cosine(j * k) * plus[j - 1]
            term = sine(j * k) * minus[j - 1]
            im = -term if im is None else im - term
        turn_c = table_ref[0, k : k + 1, :]
        turn_s = table_ref[1, k : k + 1, :]
        real.append(re * turn_c + im * turn_s)
        imag.append(im * turn_c - re * turn_s)
    stacked = jnp.concatenate(
        [jnp.concatenate(real, axis=0), jnp.concatenate(imag, axis=0)], axis=1
    )
    high, low = high_ref[...], low_ref[...]
    spectra = split_dot(stacked, high, low)
    square, keep = square_ref[:rows], keep_ref[:rows]
    damped_re, damped_im = [], []
    for k in range(HALF):
        damp = jnp.maximum(0.0, 1.0 - square * table_ref[2, k : k + 1, :])
        damp = damp * (keep * table_ref[3, k : k + 1, :])
        damped_re.append(spectra[rows * k : rows * (k + 1), :LANES] * damp)
        damped_im.append(spectra[rows * k : rows * (k + 1), LANES:] * -damp)
    damped = jnp.concatenate(
        [jnp.concatenate(damped_re, axis=0), jnp.concatenate(damped_im, axis=0)], axis=1
    )
    back = split_dot(damped, high, low)
    first = back[:rows, :LANES]
    real, imag = [], []
    for k in range(1, HALF):
        re = back[rows * k : rows * (k + 1), :LANES]
        im = back[rows * k : rows * (k + 1), LANES:]
        turn_c = table_ref[0, k : k + 1, :]
        turn_s = table_ref[1, k : k + 1, :]
        real.append(re * turn_c + im * turn_s)
        imag.append(re * turn_s - im * turn_c)
    out = [blocks[0] - (first + ((real[0] + real[1]) + (real[2] + real[3])))] + [None] * (RADIX - 1)
    for n in range(1, HALF):
        even = first
        odd = None
        for k in range(1, HALF):
            even = even + cosine(n * k) * real[k - 1]
            term = sine(n * k) * imag[k - 1]
            odd = term if odd is None else odd + term
        out[n] = blocks[n] - (even - odd)
        out[RADIX - n] = blocks[RADIX - n] - (even + odd)
    return out


def face_weights(courant):
    up = jnp.maximum(courant, 0.0)
    down = jnp.minimum(courant, 0.0)
    a = 0.25 * up * (1.0 - up)
    d = 0.25 * down * (1.0 + down)
    return a, up + d, down + a, d


def advect_rows(count, row_of, store, u_ref, v_ref, weight_ref):
    for r in range(count):
        u_ref[r : r + 1, :] = row_of(r)[0:1]
    for r in range(-1, count + 1):
        v_ref[r + 1 : r + 2, :] = row_of(r)[1:2]
    u = COEF * u_ref[:count]
    a, b, c, d = face_weights(0.5 * (u + pltpu.roll(u, LON - 1, 1)))
    back = lambda x: pltpu.roll(x, 1, 1)
    weight_ref[0, :count] = -back(a)
    weight_ref[1, :count] = a + back(b)
    weight_ref[3, :count] = -(c + back(d))
    weight_ref[4, :count] = d
    center = 1.0 - (b - back(c))
    a, b, c, d = face_weights((0.5 * COEF) * (v_ref[: count + 1] + v_ref[1 : count + 2]))
    weight_ref[5, :count] = -a[:count]
    weight_ref[6, :count] = a[1:] + b[:count]
    weight_ref[2, :count] = center - (b[1:] - c[:count])
    weight_ref[7, :count] = -(c[1:] + d[:count])
    weight_ref[8, :count] = d[1:]
    for r in range(count):
        weight = lambda n: weight_ref[n, r : r + 1, :]
        q = row_of(r)
        new = weight(2) * q
        for n, step in ((0, 2), (1, 1), (3, LON - 1), (4, LON - 2)):
            new = new + weight(n) * pltpu.roll(q, step, 1)
        for n, step in ((5, -2), (6, -1), (7, 1), (8, 2)):
            new = new + weight(n) * row_of(r + step)
        store(r, new)


def pack_kernel(
    mask_hbm, cutoff_hbm, winds_hbm, fields_hbm, thick_hbm, mine_ref, other_ref,
    mask_ref, cutoff_ref, winds_ref, fields_ref, thick_ref, sems,
):
    copies = [
        pltpu.make_async_copy(source, target, sems.at[i])
        for i, (source, target) in enumerate(
            (
                (mask_hbm, mask_ref), (cutoff_hbm, cutoff_ref),
                (winds_hbm, winds_ref), (fields_hbm, fields_ref), (thick_hbm, thick_ref),
            )
        )
    ]
    for copy in copies:
        copy.start()
    half = lax.axis_index("half")
    copies[0].wait()
    copies[1].wait()
    for ref in (mine_ref, other_ref):
        for r in range(ROWS):
            cut = cutoff_ref[r].astype(jnp.float32)
            ref[ROWS * RADIX, r : r + 1, :] = jnp.full((1, LANES), cut * cut, jnp.float32)
            ref[ROWS * RADIX, ROWS + r : ROWS + r + 1, :] = jnp.full(
                (1, LANES), mask_ref[r].astype(jnp.float32), jnp.float32
            )
    for copy in copies[2:]:
        copy.wait()
    for ref, level in ((mine_ref, half), (other_ref, 1 - half)):
        for f in range(8):
            for r in range(ROWS):
                if f < 2:
                    row = winds_ref[f, level, r : r + 1, :]
                elif f == 2:
                    row = thick_ref[level, r : r + 1, :]
                else:
                    row = fields_ref[f - 3, level, r : r + 1, :]
                for b in range(RADIX):
                    ref[RADIX * r + b, f : f + 1, :] = row[:, LANES * b : LANES * (b + 1)]


def unpack_rows(parts, start_ref, meta_ref):
    for ref, group in parts:
        for r in range(ROWS):
            for b in range(RADIX):
                start_ref[ROWS * group + r, :, LANES * b : LANES * (b + 1)] = ref[RADIX * r + b]
        meta_ref[group] = ref[ROWS * RADIX]


def substep(count, row_of, meta_of, limit, target_ref, tables, work):
    wind_ref, square_ref, keep_ref, u_ref, v_ref, weight_ref = work

    def store(r, new):
        new = limit(r, new)
        target_ref[r] = new
        wind_ref[2 * r : 2 * r + 2, :] = new[0:2]

    advect_rows(count, row_of, store, u_ref, v_ref, weight_ref)
    for r in range(count):
        for ref, value in zip((square_ref, keep_ref), meta_of(r)):
            ref[2 * r : 2 * r + 2, :] = jnp.broadcast_to(value, (2, LANES))
    blocks = polar_filter(2 * count, wind_ref, square_ref, keep_ref, *tables)
    for j in range(RADIX):
        for r in range(count):
            target_ref[r, 0:2, LANES * j : LANES * (j + 1)] = blocks[j][2 * r : 2 * r + 2]


def meta_rows(meta_ref, first):
    def meta_of(r):
        group, at = (first + r) // ROWS, (first + r) % ROWS
        return meta_ref[group, at : at + 1, :], meta_ref[group, ROWS + at : ROWS + at + 1, :]

    return meta_of


def outside(r, count, edge):
    half = lax.axis_index("half")
    pair = lax.axis_index("pair")
    if r < 2:
        return jnp.logical_and(half == edge, pair == 0)
    if r >= count - 2:
        return jnp.logical_and(half == 1 - edge, pair == lax.axis_size("pair") - 1)
    return None


def limiter(count, edge):
    def limit(r, new):
        beyond = outside(r, count, edge)
        return new if beyond is None else jnp.where(beyond, 0.0, new)

    return limit


def pack_band(final_ref, put, turned_ref):
    group = lax.broadcasted_iota(jnp.int32, (8, LANES), 1) // EXTRA
    extras = [None] * 8
    for r in range(ROWS):
        blocks = [final_ref[r, :, LANES * b : LANES * (b + 1)] for b in range(RADIX)]
        for owner in range(8):
            value = jnp.where(
                group < 8 - owner, turn(blocks[owner], -owner), turn(blocks[owner + 1], -owner)
            )
            turned_ref[pl.ds(32 * owner + r, 8, stride=4), :] = value
            extra = turn(blocks[owner + 1], r - owner)
            extras[owner] = extra if r == 0 else jnp.where(group == r, extra, extras[owner])
    for owner in range(8):
        put(owner, 8, jnp.where(group[:4] < 4, extras[owner][:4], swap(extras[owner])[4:]))
        for f in range(8):
            put(owner, f, turned_ref[32 * owner + 4 * f : 32 * owner + 4 * f + 4, :])


def early_kernel(
    mine_ref, partner_ref, near_ref, table_ref, high_ref, low_ref, early_ref, band_ref,
    start_ref, meta_ref, final_ref, turned_ref, *work,
):
    half = lax.axis_index("half")
    tables = (table_ref, high_ref, low_ref)
    unpack_rows(
        ((mine_ref, 2 * half), (partner_ref, 1), (near_ref, 2 - 2 * half)), start_ref, meta_ref
    )
    substep(
        2 * ROWS, lambda r: start_ref[r + 2], meta_rows(meta_ref, 2), limiter(2 * ROWS, 1),
        early_ref, tables, work,
    )
    substep(
        ROWS, lambda r: early_ref[r + 2], meta_rows(meta_ref, ROWS), lambda r, new: new, final_ref,
        tables, work,
    )

    def put(owner, tile, value):
        band_ref[owner, tile] = value

    pack_band(final_ref, put, turned_ref)


def late_kernel(
    mine_ref, far_ref, early_ref, band_ref, table_ref, high_ref, low_ref, send_ref,
    start_ref, meta_ref, rest_ref, first_ref, final_ref, turned_ref, *work,
):
    half = lax.axis_index("half")
    tables = (table_ref, high_ref, low_ref)
    for owner in range(8):
        send_ref[8 * (1 - half) + owner] = band_ref[owner]
    for r in range(ROWS):
        first_ref[ROWS * (1 - half) + r] = early_ref[ROWS * half + r]
    unpack_rows(((mine_ref, 1 - half), (far_ref, half)), start_ref, meta_ref)
    substep(
        ROWS, lambda r: start_ref[r + 2], meta_rows(meta_ref, 2), limiter(ROWS, 0), rest_ref, tables,
        work,
    )
    for r in range(ROWS):
        first_ref[ROWS * half + r] = rest_ref[r]
    meta_ref[0] = mine_ref[ROWS * RADIX]
    substep(
        ROWS, lambda r: first_ref[r + 2], meta_rows(meta_ref, 0), lambda r, new: new, final_ref,
        tables, work,
    )

    def put(owner, tile, value):
        send_ref[8 * half + owner, tile] = value

    pack_band(final_ref, put, turned_ref)


def turn(x, steps):
    return pltpu.roll(x, EXTRA * (steps % 8), 1) if steps % 8 else x


def swap(x):
    return turn(x, 4)


def tile_of(f, level):
    return 7 * level + (f if f < 2 else f - 1)


def remap_kernel(got_ref, send_ref, mass_ref, edge_ref):
    levels = 16
    pairs = ((0, 1), (3, 4), (5, 6), (7, 7))
    both = lambda source, a, b: jnp.concatenate([got_ref[source, a], got_ref[source, b]], axis=0)
    inside = lambda lower, upper, low, high: jnp.maximum(
        0.0, jnp.minimum(upper, high) - jnp.maximum(lower, low)
    )
    add = lambda total, term: term if total is None else total + term

    edges = [jnp.zeros((8, LANES), jnp.float32)]
    for k in range(levels):
        edges.append(edges[-1] + both(8 * (k % 2) + k // 2, 2, 2))
    mass = edges[-1]
    scale = float(levels) / mass
    for i in range(levels + 1):
        edge_ref[i] = edges[i]
    chunk = 8
    for first in range(0, levels, chunk):
        bounds = [mass * (m / levels) for m in range(first, first + chunk + 1)]
        totals = [[None] * len(pairs) for _ in range(chunk)]
        for k in range(levels):
            lower, upper = edge_ref[k], edge_ref[k + 1]
            values = [both(8 * (k % 2) + k // 2, a, b) for a, b in pairs]
            for m in range(chunk):
                overlap = inside(lower, upper, bounds[m], bounds[m + 1])
                for p, value in enumerate(values):
                    totals[m][p] = add(totals[m][p], value * overlap)
        for m in range(chunk):
            target, level = (first + m) // 2, (first + m) % 2
            for p, (a, b) in enumerate(pairs):
                total = totals[m][p] * scale
                send_ref[target, tile_of(a, level)] = total[:4]
                if b != a:
                    send_ref[target, tile_of(b, level)] = total[4:]
    mass_ref[:, :LANES] = mass[:4]

    left = lax.broadcasted_iota(jnp.int32, (8, LANES), 1) < LANES // 2
    base = jnp.zeros((8, LANES), jnp.float32)
    steps = []
    for k in range(levels // 2):
        even, odd = got_ref[k, 8], got_ref[8 + k, 8]
        value = jnp.concatenate(
            [jnp.where(left[:4], even, swap(odd)), jnp.where(left[:4], swap(even), odd)], axis=0
        )
        thick = jnp.broadcast_to(value[2:3], (8, LANES))
        other = swap(thick)
        lower = base + jnp.where(left, 0.0, other)
        upper = lower + thick
        base = jnp.where(left, upper + other, upper)
        steps.append((value, lower, upper))
    scale = float(levels) / base
    bounds = [base * (m / levels) for m in range(levels + 1)]
    totals = [None] * levels
    for value, lower, upper in steps:
        for m in range(levels):
            totals[m] = add(totals[m], value * inside(lower, upper, bounds[m], bounds[m + 1]))
    totals = [(total + swap(total)) * scale for total in totals]
    for m in range(0, levels, 2):
        mixed = jnp.where(left, totals[m], totals[m + 1])
        send_ref[m // 2, TILES - 2] = mixed[:4]
        send_ref[m // 2, TILES - 1] = mixed[4:]
    for r in range(ROWS):
        mass_ref[r : r + 1, LANES:] = turn(base, -r)[0:1, :EXTRA]


def unpack_kernel(got_ref, winds_ref, fields_ref, extra_ref):
    extras = [
        jnp.concatenate([got_ref[owner, TILES - 2], got_ref[owner, TILES - 1]], axis=0)
        for owner in range(8)
    ]
    group = lax.broadcasted_iota(jnp.int32, (8, LANES), 1) // EXTRA
    for l in range(2):
        for r in range(ROWS):
            value = turn(extras[0], -4 * l - r)
            for owner in range(1, 8):
                value = jnp.where(group == owner, turn(extras[owner], owner - 4 * l - r), value)
            extra_ref[pl.ds(32 * l + r, 8, stride=4), :] = value
    group = group[:4]
    for f in range(8):
        if f == 2:
            continue
        for l in range(2):
            ref, at = (winds_ref, f) if f < 2 else (fields_ref, f - 3)
            extra = extra_ref[32 * l + 4 * f : 32 * l + 4 * f + 4, :]
            turned = [turn(got_ref[owner, tile_of(f, l)], owner) for owner in range(8)]
            for b in range(RADIX):
                if b == 0:
                    value = turned[0]
                else:
                    value = jnp.where(group == b - 1, extra, turned[b - 1])
                    if b < 8:
                        value = jnp.where(group < b, value, turned[b])
                ref[at, l, :, LANES * b : LANES * (b + 1)] = value


VMEM = pl.BlockSpec(memory_space=pltpu.VMEM)
HBM = pl.BlockSpec(memory_space=pltpu.HBM)
PARAMS = pltpu.CompilerParams(vmem_limit_bytes=24 * 1024 * 1024)


def shape(*sizes):
    return jax.ShapeDtypeStruct(sizes, jnp.float32)


def scratch(*sizes):
    return pltpu.VMEM(sizes, jnp.float32)


def shards(winds, fields, thickness, filter_mask, cutoff):
    table, high, low = (jnp.asarray(x) for x in make_tables())
    pairs = lax.axis_size("pair")
    mine, other = pl.pallas_call(
        pack_kernel,
        out_shape=[pltpu.VMEM((ROWS * RADIX + 1, 8, LANES), jnp.float32)] * 2,
        in_specs=[HBM] * 5,
        out_specs=[VMEM] * 2,
        scratch_shapes=[
            pltpu.SMEM((ROWS,), jnp.int32), pltpu.SMEM((ROWS,), jnp.int32),
            scratch(*winds.shape), scratch(*fields.shape), scratch(*thickness.shape),
            pltpu.SemaphoreType.DMA((5,)),
        ],
        compiler_params=pltpu.CompilerParams(vmem_limit_bytes=60 * 1024 * 1024),
    )(filter_mask, cutoff, winds, fields, thickness)
    bands = ("pair", "half")
    ups = [(2 * p + 1, 2 * p + 3) for p in range(pairs - 1)]
    downs = [(2 * p, 2 * p - 2) for p in range(1, pairs)]
    near = lax.ppermute(mine, bands, ups + downs)
    partner = lax.ppermute(other, bands, [(i, i ^ 1) for i in range(2 * pairs)])
    ups = [(2 * p, 2 * p + 2) for p in range(pairs - 1)]
    downs = [(2 * p + 1, 2 * p - 1) for p in range(1, pairs)]
    far = lax.ppermute(partner, bands, ups + downs)
    work = [
        scratch(16, LON), scratch(16, LANES), scratch(16, LANES), scratch(8, LON), scratch(16, LON),
        scratch(9, 8, LON),
    ]
    early, band = pl.pallas_call(
        early_kernel,
        out_shape=[
            pltpu.VMEM((2 * ROWS, 8, LON), jnp.float32), pltpu.VMEM((8, 9, 4, LANES), jnp.float32)
        ],
        in_specs=[VMEM] * 6,
        out_specs=[VMEM] * 2,
        scratch_shapes=[
            scratch(3 * ROWS, 8, LON), scratch(3, 8, LANES), scratch(ROWS, 8, LON),
            scratch(256, LANES),
        ] + work,
        compiler_params=PARAMS,
        cost_estimate=pl.CostEstimate(flops=0, bytes_accessed=3_000_000, transcendentals=0),
    )(mine, partner, near, table, high, low)
    send = pl.pallas_call(
        late_kernel,
        out_shape=shape(16, 9, 4, LANES),
        in_specs=[VMEM] * 7,
        out_specs=VMEM,
        scratch_shapes=[
            scratch(2 * ROWS, 8, LON), scratch(2, 8, LANES), scratch(ROWS, 8, LON),
            scratch(2 * ROWS, 8, LON), scratch(ROWS, 8, LON), scratch(256, LANES),
        ] + work,
        compiler_params=PARAMS,
    )(mine, far, early, band, table, high, low)
    got = lax.all_to_all(send, ("half", "lev"), split_axis=0, concat_axis=0, tiled=True)
    send, mass = pl.pallas_call(
        remap_kernel,
        out_shape=[pltpu.VMEM((8, TILES, 4, LANES), jnp.float32), shape(4, LANES + EXTRA)],
        in_specs=[VMEM],
        out_specs=[VMEM] * 2,
        scratch_shapes=[scratch(17, 8, LANES)],
        compiler_params=PARAMS,
    )(got)
    got = lax.all_to_all(send, "lev", split_axis=0, concat_axis=0, tiled=True)
    winds_out, fields_out = pl.pallas_call(
        unpack_kernel,
        out_shape=[shape(2, 2, 4, LON), shape(5, 2, 4, LON)],
        in_specs=[VMEM],
        out_specs=[VMEM] * 2,
        scratch_shapes=[scratch(64, LANES)],
        compiler_params=PARAMS,
    )(got)
    return winds_out, fields_out, mass


def solution(mesh):
    devices = mesh.devices
    mesh = jax.sharding.Mesh(
        devices.reshape(devices.shape[0] // 2, 2, devices.shape[1]), ("pair", "half", "lev")
    )
    lat = ("pair", "half")
    return jax.shard_map(
        shards,
        mesh=mesh,
        in_specs=(
            P(None, "lev", lat, None),
            P(None, "lev", lat, None),
            P("lev", lat, None),
            P(lat),
            P(lat),
        ),
        out_specs=(P(None, "lev", lat, None), P(None, "lev", lat, None), P(lat, "lev")),
        check_vma=False,
    )
```

profile of v0, /device:TPU:6, one launch (start us, length us, event | category | flops | bytes accessed | tf_op | source)
XLA Modules:
  0.0 61.3 jit_solution(3095613734182775051)
XLA Ops:
  0.6 0.0 copy-start
  0.6 0.0 copy-start.1
  0.7 0.0 copy-start.2
  0.7 1.2 %shard_map.103 = (f32[37,8,128]{2,1,0:T(8,128)S(1)}, f32[37,8,128]{2,1,0:T(8,128)S(1)}) custom-call(s32[4]{0:T(128)} %mask_hbm.1, s32[4]{0:T(128)} %cutoff_hbm.1, f32[2,2,4,1152]{3,2,1,0:T(4,128)} %winds_hbm.1, f32[5,2,4,1152]{3,2,1,0:T(4,128)} %fields_hbm.1, f32[2,4,1152]{2,1,0:T(4,128)} %thick_hbm.1), custom_call_target="tpu_custom_call" | custom-call | tf_op jit(solution)/shard_map/pallas_call | solution.py:430
  1.9 4.3 %collective-permute-start = (f32[37,8,128]{2,1,0:T(8,128)S(1)}, f32[37,8,128]{2,1,0:T(8,128)S(1)}, u32[]{:S(2)}, u32[]{:S(2)}) collective-permute-start(f32[37,8,128]{2,1,0:T(8,128)S(1)} %get-tuple-element.12), channel_id=1, source_target_pairs={{0,8},{8,0},{16,24},{24,16},{32,40},{40,32},{48,56},{56,48},{64,72... | collective-permute-start | bytes 454664 | tf_op jit(solution)/shard_map/ppermute | solution.py:446
  6.2 5.6 %collective-permute-start.2 = (f32[37,8,128]{2,1,0:T(8,128)S(1)}, f32[37,8,128]{2,1,0:T(8,128)S(1)}, u32[]{:S(2)}, u32[]{:S(2)}) collective-permute-start(f32[37,8,128]{2,1,0:T(8,128)S(1)} %get-tuple-element.11.mine_ref), channel_id=1, source_target_pairs={{8,24},{24,40},{40,56},{56,72},{72,88},{88,104},{104,120},{120,136... | collective-permute-start | bytes 454664 | tf_op jit(solution)/shard_map/ppermute | solution.py:445
  11.8 0.0 collective-permute-done.partner_ref
  11.9 1.9 %collective-permute-start.1 = (f32[37,8,128]{2,1,0:T(8,128)S(1)}, f32[37,8,128]{2,1,0:T(8,128)S(1)}, u32[]{:S(2)}, u32[]{:S(2)}) collective-permute-start(f32[37,8,128]{2,1,0:T(8,128)S(1)} %collective-permute-done.partner_ref), channel_id=1, source_target_pairs={{0,16},{16,32},{32,48},{48,64},{64,80},{80,96},{96,112},{112,128},... | collective-permute-start | bytes 454664 | tf_op jit(solution)/shard_map/ppermute | solution.py:449
  13.8 1.0 %collective-permute-done.2.near_ref = f32[37,8,128]{2,1,0:T(8,128)S(1)} collective-permute-done((f32[37,8,128]{2,1,0:T(8,128)S(1)}, f32[37,8,128]{2,1,0:T(8,128)S(1)}, u32[]{:S(2)}, u32[]{:S(2)}) %collective-permute-start.2) | collective-permute-done | bytes 151584 | tf_op jit(solution)/shard_map/ppermute | solution.py:445
  14.7 0.0 copy-done
  14.7 0.0 copy-done.1
  14.7 0.0 copy-done.2
  14.7 2.1 %shard_map.104 = (f32[8,8,1152]{2,1,0:T(8,128)S(1)}, f32[8,9,4,128]{3,2,1,0:T(4,128)S(1)}) custom-call(f32[37,8,128]{2,1,0:T(8,128)S(1)} %get-tuple-element.11.mine_ref, f32[37,8,128]{2,1,0:T(8,128)S(1)} %collective-permute-done.partner_ref, f32[37,8,128]{2,1,0:T(8,128)S(1)} %collective-permute-done.2.near_ref, f32[4,8,128]{2,1,0:T(8,128)S(1)} %copy-done.2, ...), custom_call_target="tpu_custom_call" | custom-call | bytes 3000000 | tf_op jit(solution)/shard_map/pallas_call | solution.py:454
  16.8 4.2 %collective-permute-done.1.far_ref = f32[37,8,128]{2,1,0:T(8,128)S(1)} collective-permute-done((f32[37,8,128]{2,1,0:T(8,128)S(1)}, f32[37,8,128]{2,1,0:T(8,128)S(1)}, u32[]{:S(2)}, u32[]{:S(2)}) %collective-permute-start.1) | collective-permute-done | bytes 151584 | tf_op jit(solution)/shard_map/ppermute | solution.py:449
  21.0 1.9 %shard_map.105 = f32[16,9,4,128]{3,2,1,0:T(4,128)S(1)} custom-call(f32[37,8,128]{2,1,0:T(8,128)S(1)} %get-tuple-element.11.mine_ref, f32[37,8,128]{2,1,0:T(8,128)S(1)} %collective-permute-done.1.far_ref, f32[8,8,1152]{2,1,0:T(8,128)S(1)} %get-tuple-element.13.early_ref, f32[8,9,4,128]{3,2,1,0:T(4,128)S(1)} %get-tuple-element.14.band_ref, ...), custom_call_target="tpu_custom_call" | custom-call | tf_op jit(solution)/shard_map/pallas_call | solution.py:468
  22.9 21.3 %all_to_all.10.got_ref = f32[16,9,4,128]{3,2,1,0:T(4,128)S(1)} all-to-all(f32[16,9,4,128]{3,2,1,0:T(4,128)S(1)} %shard_map.105), channel_id=1, replica_groups=mesh['pair'=32,'half'=2,'lev'=8] {'half','lev'}, dimensions={0} | all-to-all | bytes 589824 | tf_op jit(solution)/shard_map/all_to_all | solution.py:479
  44.2 0.9 %shard_map.106 = (f32[8,16,4,128]{3,2,1,0:T(4,128)S(1)}, f32[4,144]{1,0:T(4,128)}) custom-call(f32[16,9,4,128]{3,2,1,0:T(4,128)S(1)} %all_to_all.10.got_ref), custom_call_target="tpu_custom_call" | custom-call | tf_op jit(solution)/shard_map/pallas_call | solution.py:480
  45.1 15.2 %all_to_all.11.got_ref = f32[8,16,4,128]{3,2,1,0:T(4,128)S(1)} all-to-all(f32[8,16,4,128]{3,2,1,0:T(4,128)S(1)} %get-tuple-element.15), channel_id=1, replica_groups=mesh['pair'=32,'half'=2,'lev'=8] {'lev'}, dimensions={0} | all-to-all | bytes 524288 | tf_op jit(solution)/shard_map/all_to_all | solution.py:488
  60.4 0.9 %shard_map.107 = (f32[2,2,4,1152]{3,2,1,0:T(4,128)}, f32[5,2,4,1152]{3,2,1,0:T(4,128)}) custom-call(f32[8,16,4,128]{3,2,1,0:T(4,128)S(1)} %all_to_all.11.got_ref), custom_call_target="tpu_custom_call" | custom-call | tf_op jit(solution)/shard_map/pallas_call | solution.py:489
Async XLA Ops:
  0.6 14.1 %copy-start = (bf16[256,256]{1,0:T(8,128)(2,1)S(1)}, bf16[256,256]{1,0:T(8,128)(2,1)}, u32[]{:S(2)}) copy-start(bf16[256,256]{1,0:T(8,128)(2,1)} %constant.7.clone.high_ref) | copy-start | bytes 393220
  0.6 14.1 %copy-start.1 = (bf16[256,256]{1,0:T(8,128)(2,1)S(1)}, bf16[256,256]{1,0:T(8,128)(2,1)}, u32[]{:S(2)}) copy-start(bf16[256,256]{1,0:T(8,128)(2,1)} %constant.8.clone.low_ref) | copy-start | bytes 393220
  0.7 14.1 %copy-start.2 = (f32[4,8,128]{2,1,0:T(8,128)S(1)}, f32[4,8,128]{2,1,0:T(8,128)}, u32[]{:S(2)}) copy-start(f32[4,8,128]{2,1,0:T(8,128)} %constant.6.clone.table_ref) | copy-start | bytes 49156
  1.9 9.9 %collective-permute-start = (f32[37,8,128]{2,1,0:T(8,128)S(1)}, f32[37,8,128]{2,1,0:T(8,128)S(1)}, u32[]{:S(2)}, u32[]{:S(2)}) collective-permute-start(f32[37,8,128]{2,1,0:T(8,128)S(1)} %get-tuple-element.12), channel_id=1, source_target_pairs={{0,8},{8,0},{16,24},{24,16},{32,40},{40,32},{48,56},{56,48},{64,72... | collective-permute-start | bytes 454664 | tf_op jit(solution)/shard_map/ppermute | solution.py:446
  6.2 8.5 %collective-permute-start.2 = (f32[37,8,128]{2,1,0:T(8,128)S(1)}, f32[37,8,128]{2,1,0:T(8,128)S(1)}, u32[]{:S(2)}, u32[]{:S(2)}) collective-permute-start(f32[37,8,128]{2,1,0:T(8,128)S(1)} %get-tuple-element.11.mine_ref), channel_id=1, source_target_pairs={{8,24},{24,40},{40,56},{56,72},{72,88},{88,104},{104,120},{120,136... | collective-permute-start | bytes 454664 | tf_op jit(solution)/shard_map/ppermute | solution.py:445
  11.9 9.2 %collective-permute-start.1 = (f32[37,8,128]{2,1,0:T(8,128)S(1)}, f32[37,8,128]{2,1,0:T(8,128)S(1)}, u32[]{:S(2)}, u32[]{:S(2)}) collective-permute-start(f32[37,8,128]{2,1,0:T(8,128)S(1)} %collective-permute-done.partner_ref), channel_id=1, source_target_pairs={{0,16},{16,32},{32,48},{48,64},{64,80},{80,96},{96,112},{112,128},... | collective-permute-start | bytes 454664 | tf_op jit(solution)/shard_map/ppermute | solution.py:449
where the time goes:
time: 61.5 us; the launch traced here: 61.3 us
  blocking collectives  36.5 us (59%)
  starting transfers between devices  11.8 us (19%)
  Pallas kernels  7.05 us (11%)
  waiting for transfers between devices  5.15 us (8%)
  between operations  0.71 us (1%)
    all_to_all x1, blocking collectives, shards(): lax.all_to_all(send, ('half', 'lev'), split_axis=0, concat_axis=0, tiled=...  21.3 us
    all_to_all x1, blocking collectives, shards(): got = lax.all_to_all(send, 'lev', split_axis=0, concat_axis=0, tiled=True)  15.2 us
    ppermute x1, starting transfers between devices, shards(): near = lax.ppermute(mine, bands, ups + downs)  5.64 us
    ppermute x1, starting transfers between devices, shards(): partner = lax.ppermute(other, bands, [(i, i ^ 1) for i in range(2 * pairs)])  4.28 us
    ppermute x1, waiting for transfers between devices, shards(): far = lax.ppermute(partner, bands, ups + downs)  4.2 us
    pallas_call x1, Pallas kernels, shards(): pl.pallas_call(early_kernel, out_shape=[pltpu.VMEM((2 * ROWS, 8, LON), jn...  2.1 us
    ppermute x1, starting transfers between devices, shards(): far = lax.ppermute(partner, bands, ups + downs)  1.92 us
    pallas_call x1, Pallas kernels, shards(): pl.pallas_call(late_kernel, out_shape=shape(16, 9, 4, LANES), in_specs=[V...  1.88 us
  transfers between devices with their start and end apart: 3, of which 2 were waited for; matrix products, arithmetic and copies ran while one was open for 0% of the time, Pallas kernels for 3%

commit v1 on v0

--- a/solution.py
+++ b/solution.py
@@ -41,10 +41,13 @@
 
 
 def split_dot(left, high, low):
+    rows = left.shape[0]
     left_high = left.astype(jnp.bfloat16)
-    left_low = (left - left_high.astype(jnp.float32)).astype(jnp.bfloat16)
+    coarse = left_high.astype(jnp.float32)
+    stacked = jnp.concatenate([coarse, left - coarse], axis=0).astype(jnp.bfloat16)
     dot = lambda a, b: jnp.dot(a, b, preferred_element_type=jnp.float32)
-    return dot(left_high, high) + (dot(left_low, high) + dot(left_high, low))
+    both = dot(stacked, high)
+    return both[:rows] + (both[rows:] + dot(left_high, low))
 
 
 def polar_filter(rows, wind_ref, square_ref, keep_ref, table_ref, high_ref, low_ref):

time: 61.5 us -> 61.4 us (level)
  no operation moved by 1% of the time
where the time goes in v1:
time: 61.4 us; the launch traced here: 61.1 us
  blocking collectives  36.5 us (59%)
  starting transfers between devices  11.8 us (19%)
  Pallas kernels  6.79 us (11%)
  waiting for transfers between devices  5.27 us (9%)
  between operations  0.7 us (1%)
    all_to_all x1, blocking collectives, shards(): lax.all_to_all(send, ('half', 'lev'), split_axis=0, concat_axis=0, tiled=...  21.3 us
    all_to_all x1, blocking collectives, shards(): got = lax.all_to_all(send, 'lev', split_axis=0, concat_axis=0, tiled=True)  15.2 us
    ppermute x1, starting transfers between devices, shards(): near = lax.ppermute(mine, bands, ups + downs)  5.64 us
    ppermute x1, waiting for transfers between devices, shards(): far = lax.ppermute(partner, bands, ups + downs)  4.31 us
    ppermute x1, starting transfers between devices, shards(): partner = lax.ppermute(other, bands, [(i, i ^ 1) for i in range(2 * pairs)])  4.28 us
    pallas_call x1, Pallas kernels, shards(): pl.pallas_call(early_kernel, out_shape=[pltpu.VMEM((2 * ROWS, 8, LON), jn...  1.99 us
    ppermute x1, starting transfers between devices, shards(): far = lax.ppermute(partner, bands, ups + downs)  1.92 us
    pallas_call x1, Pallas kernels, shards(): pl.pallas_call(late_kernel, out_shape=shape(16, 9, 4, LANES), in_specs=[V...  1.72 us
  transfers between devices with their start and end apart: 3, of which 2 were waited for; matrix products, arithmetic and copies ran while one was open for 0% of the time, Pallas kernels for 3%

profile of v1, /device:TPU:6, one launch (start us, length us, event | category | flops | bytes accessed | tf_op | source)
XLA Modules:
  0.0 61.1 jit_solution(16361581391958447499)
XLA Ops:
  0.6 0.0 copy-start
  0.6 0.0 copy-start.1
  0.7 0.0 copy-start.2
  0.7 1.2 %shard_map.103 = (f32[37,8,128]{2,1,0:T(8,128)S(1)}, f32[37,8,128]{2,1,0:T(8,128)S(1)}) custom-call(s32[4]{0:T(128)} %mask_hbm.1, s32[4]{0:T(128)} %cutoff_hbm.1, f32[2,2,4,1152]{3,2,1,0:T(4,128)} %winds_hbm.1, f32[5,2,4,1152]{3,2,1,0:T(4,128)} %fields_hbm.1, f32[2,4,1152]{2,1,0:T(4,128)} %thick_hbm.1), custom_call_target="tpu_custom_call" | custom-call | tf_op jit(solution)/shard_map/pallas_call | solution.py:433
  1.9 4.3 %collective-permute-start = (f32[37,8,128]{2,1,0:T(8,128)S(1)}, f32[37,8,128]{2,1,0:T(8,128)S(1)}, u32[]{:S(2)}, u32[]{:S(2)}) collective-permute-start(f32[37,8,128]{2,1,0:T(8,128)S(1)} %get-tuple-element.12), channel_id=1, source_target_pairs={{0,8},{8,0},{16,24},{24,16},{32,40},{40,32},{48,56},{56,48},{64,72... | collective-permute-start | bytes 454664 | tf_op jit(solution)/shard_map/ppermute | solution.py:449
  6.2 5.6 %collective-permute-start.2 = (f32[37,8,128]{2,1,0:T(8,128)S(1)}, f32[37,8,128]{2,1,0:T(8,128)S(1)}, u32[]{:S(2)}, u32[]{:S(2)}) collective-permute-start(f32[37,8,128]{2,1,0:T(8,128)S(1)} %get-tuple-element.11.mine_ref), channel_id=1, source_target_pairs={{8,24},{24,40},{40,56},{56,72},{72,88},{88,104},{104,120},{120,136... | collective-permute-start | bytes 454664 | tf_op jit(solution)/shard_map/ppermute | solution.py:448
  11.8 0.0 collective-permute-done.partner_ref
  11.9 1.9 %collective-permute-start.1 = (f32[37,8,128]{2,1,0:T(8,128)S(1)}, f32[37,8,128]{2,1,0:T(8,128)S(1)}, u32[]{:S(2)}, u32[]{:S(2)}) collective-permute-start(f32[37,8,128]{2,1,0:T(8,128)S(1)} %collective-permute-done.partner_ref), channel_id=1, source_target_pairs={{0,16},{16,32},{32,48},{48,64},{64,80},{80,96},{96,112},{112,128},... | collective-permute-start | bytes 454664 | tf_op jit(solution)/shard_map/ppermute | solution.py:452
  13.8 1.0 %collective-permute-done.2.near_ref = f32[37,8,128]{2,1,0:T(8,128)S(1)} collective-permute-done((f32[37,8,128]{2,1,0:T(8,128)S(1)}, f32[37,8,128]{2,1,0:T(8,128)S(1)}, u32[]{:S(2)}, u32[]{:S(2)}) %collective-permute-start.2) | collective-permute-done | bytes 151584 | tf_op jit(solution)/shard_map/ppermute | solution.py:448
  14.7 0.0 copy-done
  14.7 0.0 copy-done.1
  14.7 0.0 copy-done.2
  14.7 2.0 %shard_map.104 = (f32[8,8,1152]{2,1,0:T(8,128)S(1)}, f32[8,9,4,128]{3,2,1,0:T(4,128)S(1)}) custom-call(f32[37,8,128]{2,1,0:T(8,128)S(1)} %get-tuple-element.11.mine_ref, f32[37,8,128]{2,1,0:T(8,128)S(1)} %collective-permute-done.partner_ref, f32[37,8,128]{2,1,0:T(8,128)S(1)} %collective-permute-done.2.near_ref, f32[4,8,128]{2,1,0:T(8,128)S(1)} %copy-done.2, ...), custom_call_target="tpu_custom_call" | custom-call | bytes 3000000 | tf_op jit(solution)/shard_map/pallas_call | solution.py:457
  16.7 4.3 %collective-permute-done.1.far_ref = f32[37,8,128]{2,1,0:T(8,128)S(1)} collective-permute-done((f32[37,8,128]{2,1,0:T(8,128)S(1)}, f32[37,8,128]{2,1,0:T(8,128)S(1)}, u32[]{:S(2)}, u32[]{:S(2)}) %collective-permute-start.1) | collective-permute-done | bytes 151584 | tf_op jit(solution)/shard_map/ppermute | solution.py:452
  21.0 1.7 %shard_map.105 = f32[16,9,4,128]{3,2,1,0:T(4,128)S(1)} custom-call(f32[37,8,128]{2,1,0:T(8,128)S(1)} %get-tuple-element.11.mine_ref, f32[37,8,128]{2,1,0:T(8,128)S(1)} %collective-permute-done.1.far_ref, f32[8,8,1152]{2,1,0:T(8,128)S(1)} %get-tuple-element.13.early_ref, f32[8,9,4,128]{3,2,1,0:T(4,128)S(1)} %get-tuple-element.14.band_ref, ...), custom_call_target="tpu_custom_call" | custom-call | tf_op jit(solution)/shard_map/pallas_call | solution.py:471
  22.8 21.3 %all_to_all.10.got_ref = f32[16,9,4,128]{3,2,1,0:T(4,128)S(1)} all-to-all(f32[16,9,4,128]{3,2,1,0:T(4,128)S(1)} %shard_map.105), channel_id=1, replica_groups=mesh['pair'=32,'half'=2,'lev'=8] {'half','lev'}, dimensions={0} | all-to-all | bytes 589824 | tf_op jit(solution)/shard_map/all_to_all | solution.py:482
  44.0 0.9 %shard_map.106 = (f32[8,16,4,128]{3,2,1,0:T(4,128)S(1)}, f32[4,144]{1,0:T(4,128)}) custom-call(f32[16,9,4,128]{3,2,1,0:T(4,128)S(1)} %all_to_all.10.got_ref), custom_call_target="tpu_custom_call" | custom-call | tf_op jit(solution)/shard_map/pallas_call | solution.py:483
  45.0 15.2 %all_to_all.11.got_ref = f32[8,16,4,128]{3,2,1,0:T(4,128)S(1)} all-to-all(f32[8,16,4,128]{3,2,1,0:T(4,128)S(1)} %get-tuple-element.15), channel_id=1, replica_groups=mesh['pair'=32,'half'=2,'lev'=8] {'lev'}, dimensions={0} | all-to-all | bytes 524288 | tf_op jit(solution)/shard_map/all_to_all | solution.py:491
  60.2 0.9 %shard_map.107 = (f32[2,2,4,1152]{3,2,1,0:T(4,128)}, f32[5,2,4,1152]{3,2,1,0:T(4,128)}) custom-call(f32[8,16,4,128]{3,2,1,0:T(4,128)S(1)} %all_to_all.11.got_ref), custom_call_target="tpu_custom_call" | custom-call | tf_op jit(solution)/shard_map/pallas_call | solution.py:492
Async XLA Ops:
  0.6 14.1 %copy-start = (bf16[256,256]{1,0:T(8,128)(2,1)S(1)}, bf16[256,256]{1,0:T(8,128)(2,1)}, u32[]{:S(2)}) copy-start(bf16[256,256]{1,0:T(8,128)(2,1)} %constant.7.clone.high_ref) | copy-start | bytes 393220
  0.6 14.1 %copy-start.1 = (bf16[256,256]{1,0:T(8,128)(2,1)S(1)}, bf16[256,256]{1,0:T(8,128)(2,1)}, u32[]{:S(2)}) copy-start(bf16[256,256]{1,0:T(8,128)(2,1)} %constant.8.clone.low_ref) | copy-start | bytes 393220
  0.7 14.1 %copy-start.2 = (f32[4,8,128]{2,1,0:T(8,128)S(1)}, f32[4,8,128]{2,1,0:T(8,128)}, u32[]{:S(2)}) copy-start(f32[4,8,128]{2,1,0:T(8,128)} %constant.6.clone.table_ref) | copy-start | bytes 49156
  1.9 9.9 %collective-permute-start = (f32[37,8,128]{2,1,0:T(8,128)S(1)}, f32[37,8,128]{2,1,0:T(8,128)S(1)}, u32[]{:S(2)}, u32[]{:S(2)}) collective-permute-start(f32[37,8,128]{2,1,0:T(8,128)S(1)} %get-tuple-element.12), channel_id=1, source_target_pairs={{0,8},{8,0},{16,24},{24,16},{32,40},{40,32},{48,56},{56,48},{64,72... | collective-permute-start | bytes 454664 | tf_op jit(solution)/shard_map/ppermute | solution.py:449
  6.2 8.5 %collective-permute-start.2 = (f32[37,8,128]{2,1,0:T(8,128)S(1)}, f32[37,8,128]{2,1,0:T(8,128)S(1)}, u32[]{:S(2)}, u32[]{:S(2)}) collective-permute-start(f32[37,8,128]{2,1,0:T(8,128)S(1)} %get-tuple-element.11.mine_ref), channel_id=1, source_target_pairs={{8,24},{24,40},{40,56},{56,72},{72,88},{88,104},{104,120},{120,136... | collective-permute-start | bytes 454664 | tf_op jit(solution)/shard_map/ppermute | solution.py:448
  11.9 9.2 %collective-permute-start.1 = (f32[37,8,128]{2,1,0:T(8,128)S(1)}, f32[37,8,128]{2,1,0:T(8,128)S(1)}, u32[]{:S(2)}, u32[]{:S(2)}) collective-permute-start(f32[37,8,128]{2,1,0:T(8,128)S(1)} %collective-permute-done.partner_ref), channel_id=1, source_target_pairs={{0,16},{16,32},{32,48},{48,64},{64,80},{80,96},{96,112},{112,128},... | collective-permute-start | bytes 454664 | tf_op jit(solution)/shard_map/ppermute | solution.py:452

commit v2 on v1

--- a/solution.py
+++ b/solution.py
@@ -285,7 +285,7 @@
     half = lax.axis_index("half")
     tables = (table_ref, high_ref, low_ref)
     for owner in range(8):
-        send_ref[8 * (1 - half) + owner] = band_ref[owner]
+        send_ref[2 * owner + 1 - half] = band_ref[owner]
     for r in range(ROWS):
         first_ref[ROWS * (1 - half) + r] = early_ref[ROWS * half + r]
     unpack_rows(((mine_ref, 1 - half), (far_ref, half)), start_ref, meta_ref)
@@ -302,7 +302,7 @@
     )
 
     def put(owner, tile, value):
-        send_ref[8 * half + owner, tile] = value
+        send_ref[2 * owner + half, tile] = value
 
     pack_band(final_ref, put, turned_ref)
 
@@ -330,7 +330,7 @@
 
     edges = [jnp.zeros((8, LANES), jnp.float32)]
     for k in range(levels):
-        edges.append(edges[-1] + both(8 * (k % 2) + k // 2, 2, 2))
+        edges.append(edges[-1] + both(k, 2, 2))
     mass = edges[-1]
     scale = float(levels) / mass
     for i in range(levels + 1):
@@ -341,7 +341,7 @@
         totals = [[None] * len(pairs) for _ in range(chunk)]
         for k in range(levels):
             lower, upper = edge_ref[k], edge_ref[k + 1]
-            values = [both(8 * (k % 2) + k // 2, a, b) for a, b in pairs]
+            values = [both(k, a, b) for a, b in pairs]
             for m in range(chunk):
                 overlap = inside(lower, upper, bounds[m], bounds[m + 1])
                 for p, value in enumerate(values):
@@ -359,7 +359,7 @@
     base = jnp.zeros((8, LANES), jnp.float32)
     steps = []
     for k in range(levels // 2):
-        even, odd = got_ref[k, 8], got_ref[8 + k, 8]
+        even, odd = got_ref[2 * k, 8], got_ref[2 * k + 1, 8]
         value = jnp.concatenate(
             [jnp.where(left[:4], even, swap(odd)), jnp.where(left[:4], swap(even), odd)], axis=0
         )
@@ -479,7 +479,7 @@
         ] + work,
         compiler_params=PARAMS,
     )(mine, far, early, band, table, high, low)
-    got = lax.all_to_all(send, ("half", "lev"), split_axis=0, concat_axis=0, tiled=True)
+    got = lax.all_to_all(send, ("lev", "half"), split_axis=0, concat_axis=0, tiled=True)
     send, mass = pl.pallas_call(
         remap_kernel,
         out_shape=[pltpu.VMEM((8, TILES, 4, LANES), jnp.float32), shape(4, LANES + EXTRA)],

time: 61.4 us -> 61.9 us (level)
    all_to_all x1, blocking collectives: 15.2 us -> 16.6 us  [shards(): got = lax.all_to_all(send, 'lev', split_axis=0, concat_axis=0, tiled=True)]
    all_to_all x1, blocking collectives: 21.3 us -> 20.4 us  [shards(): lax.all_to_all(send, ('lev', 'half'), split_axis=0, concat_axis=0, tiled=...]
where the time goes in v2:
time: 61.9 us; the launch traced here: 61.6 us
  blocking collectives  37 us (60%)
  starting transfers between devices  11.8 us (19%)
  Pallas kernels  6.8 us (11%)
  waiting for transfers between devices  5.27 us (9%)
  between operations  0.71 us (1%)
    all_to_all x1, blocking collectives, shards(): lax.all_to_all(send, ('lev', 'half'), split_axis=0, concat_axis=0, tiled=...  20.4 us
    all_to_all x1, blocking collectives, shards(): got = lax.all_to_all(send, 'lev', split_axis=0, concat_axis=0, tiled=True)  16.6 us
    ppermute x1, starting transfers between devices, shards(): near = lax.ppermute(mine, bands, ups + downs)  5.64 us
    ppermute x1, waiting for transfers between devices, shards(): far = lax.ppermute(partner, bands, ups + downs)  4.31 us
    ppermute x1, starting transfers between devices, shards(): partner = lax.ppermute(other, bands, [(i, i ^ 1) for i in range(2 * pairs)])  4.28 us
    pallas_call x1, Pallas kernels, shards(): pl.pallas_call(early_kernel, out_shape=[pltpu.VMEM((2 * ROWS, 8, LON), jn...  1.99 us
    ppermute x1, starting transfers between devices, shards(): far = lax.ppermute(partner, bands, ups + downs)  1.92 us
    pallas_call x1, Pallas kernels, shards(): pl.pallas_call(late_kernel, out_shape=shape(16, 9, 4, LANES), in_specs=[V...  1.73 us
  transfers between devices with their start and end apart: 3, of which 2 were waited for; matrix products, arithmetic and copies ran while one was open for 0% of the time, Pallas kernels for 3%

profile of v2, /device:TPU:6, one launch (start us, length us, event | category | flops | bytes accessed | tf_op | source)
XLA Modules:
  0.0 61.6 jit_solution(790964789343141223)
XLA Ops:
  0.6 0.0 copy-start
  0.6 0.0 copy-start.1
  0.7 0.0 copy-start.2
  0.7 1.2 %shard_map.103 = (f32[37,8,128]{2,1,0:T(8,128)S(1)}, f32[37,8,128]{2,1,0:T(8,128)S(1)}) custom-call(s32[4]{0:T(128)} %mask_hbm.1, s32[4]{0:T(128)} %cutoff_hbm.1, f32[2,2,4,1152]{3,2,1,0:T(4,128)} %winds_hbm.1, f32[5,2,4,1152]{3,2,1,0:T(4,128)} %fields_hbm.1, f32[2,4,1152]{2,1,0:T(4,128)} %thick_hbm.1), custom_call_target="tpu_custom_call" | custom-call | tf_op jit(solution)/shard_map/pallas_call | solution.py:433
  1.9 4.3 %collective-permute-start = (f32[37,8,128]{2,1,0:T(8,128)S(1)}, f32[37,8,128]{2,1,0:T(8,128)S(1)}, u32[]{:S(2)}, u32[]{:S(2)}) collective-permute-start(f32[37,8,128]{2,1,0:T(8,128)S(1)} %get-tuple-element.12), channel_id=1, source_target_pairs={{0,8},{8,0},{16,24},{24,16},{32,40},{40,32},{48,56},{56,48},{64,72... | collective-permute-start | bytes 454664 | tf_op jit(solution)/shard_map/ppermute | solution.py:449
  6.2 5.6 %collective-permute-start.2 = (f32[37,8,128]{2,1,0:T(8,128)S(1)}, f32[37,8,128]{2,1,0:T(8,128)S(1)}, u32[]{:S(2)}, u32[]{:S(2)}) collective-permute-start(f32[37,8,128]{2,1,0:T(8,128)S(1)} %get-tuple-element.11.mine_ref), channel_id=1, source_target_pairs={{8,24},{24,40},{40,56},{56,72},{72,88},{88,104},{104,120},{120,136... | collective-permute-start | bytes 454664 | tf_op jit(solution)/shard_map/ppermute | solution.py:448
  11.8 0.0 collective-permute-done.partner_ref
  11.9 1.9 %collective-permute-start.1 = (f32[37,8,128]{2,1,0:T(8,128)S(1)}, f32[37,8,128]{2,1,0:T(8,128)S(1)}, u32[]{:S(2)}, u32[]{:S(2)}) collective-permute-start(f32[37,8,128]{2,1,0:T(8,128)S(1)} %collective-permute-done.partner_ref), channel_id=1, source_target_pairs={{0,16},{16,32},{32,48},{48,64},{64,80},{80,96},{96,112},{112,128},... | collective-permute-start | bytes 454664 | tf_op jit(solution)/shard_map/ppermute | solution.py:452
  13.8 1.0 %collective-permute-done.2.near_ref = f32[37,8,128]{2,1,0:T(8,128)S(1)} collective-permute-done((f32[37,8,128]{2,1,0:T(8,128)S(1)}, f32[37,8,128]{2,1,0:T(8,128)S(1)}, u32[]{:S(2)}, u32[]{:S(2)}) %collective-permute-start.2) | collective-permute-done | bytes 151584 | tf_op jit(solution)/shard_map/ppermute | solution.py:448
  14.7 0.0 copy-done
  14.7 0.0 copy-done.1
  14.7 0.0 copy-done.2
  14.7 2.0 %shard_map.104 = (f32[8,8,1152]{2,1,0:T(8,128)S(1)}, f32[8,9,4,128]{3,2,1,0:T(4,128)S(1)}) custom-call(f32[37,8,128]{2,1,0:T(8,128)S(1)} %get-tuple-element.11.mine_ref, f32[37,8,128]{2,1,0:T(8,128)S(1)} %collective-permute-done.partner_ref, f32[37,8,128]{2,1,0:T(8,128)S(1)} %collective-permute-done.2.near_ref, f32[4,8,128]{2,1,0:T(8,128)S(1)} %copy-done.2, ...), custom_call_target="tpu_custom_call" | custom-call | bytes 3000000 | tf_op jit(solution)/shard_map/pallas_call | solution.py:457
  16.7 4.3 %collective-permute-done.1.far_ref = f32[37,8,128]{2,1,0:T(8,128)S(1)} collective-permute-done((f32[37,8,128]{2,1,0:T(8,128)S(1)}, f32[37,8,128]{2,1,0:T(8,128)S(1)}, u32[]{:S(2)}, u32[]{:S(2)}) %collective-permute-start.1) | collective-permute-done | bytes 151584 | tf_op jit(solution)/shard_map/ppermute | solution.py:452
  21.0 1.7 %shard_map.105 = f32[16,9,4,128]{3,2,1,0:T(4,128)S(1)} custom-call(f32[37,8,128]{2,1,0:T(8,128)S(1)} %get-tuple-element.11.mine_ref, f32[37,8,128]{2,1,0:T(8,128)S(1)} %collective-permute-done.1.far_ref, f32[8,8,1152]{2,1,0:T(8,128)S(1)} %get-tuple-element.13.early_ref, f32[8,9,4,128]{3,2,1,0:T(4,128)S(1)} %get-tuple-element.14.band_ref, ...), custom_call_target="tpu_custom_call" | custom-call | tf_op jit(solution)/shard_map/pallas_call | solution.py:471
  22.8 20.4 %all_to_all.10.got_ref = f32[16,9,4,128]{3,2,1,0:T(4,128)S(1)} all-to-all(f32[16,9,4,128]{3,2,1,0:T(4,128)S(1)} %shard_map.105), channel_id=1, replica_groups=mesh['pair'=32,'half'=2,'lev'=8] {'lev','half'}, dimensions={0} | all-to-all | bytes 589824 | tf_op jit(solution)/shard_map/all_to_all | solution.py:482
  43.2 0.9 %shard_map.106 = (f32[8,16,4,128]{3,2,1,0:T(4,128)S(1)}, f32[4,144]{1,0:T(4,128)}) custom-call(f32[16,9,4,128]{3,2,1,0:T(4,128)S(1)} %all_to_all.10.got_ref), custom_call_target="tpu_custom_call" | custom-call | tf_op jit(solution)/shard_map/pallas_call | solution.py:483
  44.1 16.6 %all_to_all.11.got_ref = f32[8,16,4,128]{3,2,1,0:T(4,128)S(1)} all-to-all(f32[8,16,4,128]{3,2,1,0:T(4,128)S(1)} %get-tuple-element.15), channel_id=1, replica_groups=mesh['pair'=32,'half'=2,'lev'=8] {'lev'}, dimensions={0} | all-to-all | bytes 524288 | tf_op jit(solution)/shard_map/all_to_all | solution.py:491
  60.7 0.9 %shard_map.107 = (f32[2,2,4,1152]{3,2,1,0:T(4,128)}, f32[5,2,4,1152]{3,2,1,0:T(4,128)}) custom-call(f32[8,16,4,128]{3,2,1,0:T(4,128)S(1)} %all_to_all.11.got_ref), custom_call_target="tpu_custom_call" | custom-call | tf_op jit(solution)/shard_map/pallas_call | solution.py:492
Async XLA Ops:
  0.6 14.1 %copy-start = (bf16[256,256]{1,0:T(8,128)(2,1)S(1)}, bf16[256,256]{1,0:T(8,128)(2,1)}, u32[]{:S(2)}) copy-start(bf16[256,256]{1,0:T(8,128)(2,1)} %constant.7.clone.high_ref) | copy-start | bytes 393220
  0.6 14.1 %copy-start.1 = (bf16[256,256]{1,0:T(8,128)(2,1)S(1)}, bf16[256,256]{1,0:T(8,128)(2,1)}, u32[]{:S(2)}) copy-start(bf16[256,256]{1,0:T(8,128)(2,1)} %constant.8.clone.low_ref) | copy-start | bytes 393220
  0.7 14.1 %copy-start.2 = (f32[4,8,128]{2,1,0:T(8,128)S(1)}, f32[4,8,128]{2,1,0:T(8,128)}, u32[]{:S(2)}) copy-start(f32[4,8,128]{2,1,0:T(8,128)} %constant.6.clone.table_ref) | copy-start | bytes 49156
  1.9 9.9 %collective-permute-start = (f32[37,8,128]{2,1,0:T(8,128)S(1)}, f32[37,8,128]{2,1,0:T(8,128)S(1)}, u32[]{:S(2)}, u32[]{:S(2)}) collective-permute-start(f32[37,8,128]{2,1,0:T(8,128)S(1)} %get-tuple-element.12), channel_id=1, source_target_pairs={{0,8},{8,0},{16,24},{24,16},{32,40},{40,32},{48,56},{56,48},{64,72... | collective-permute-start | bytes 454664 | tf_op jit(solution)/shard_map/ppermute | solution.py:449
  6.2 8.5 %collective-permute-start.2 = (f32[37,8,128]{2,1,0:T(8,128)S(1)}, f32[37,8,128]{2,1,0:T(8,128)S(1)}, u32[]{:S(2)}, u32[]{:S(2)}) collective-permute-start(f32[37,8,128]{2,1,0:T(8,128)S(1)} %get-tuple-element.11.mine_ref), channel_id=1, source_target_pairs={{8,24},{24,40},{40,56},{56,72},{72,88},{88,104},{104,120},{120,136... | collective-permute-start | bytes 454664 | tf_op jit(solution)/shard_map/ppermute | solution.py:448
  11.9 9.2 %collective-permute-start.1 = (f32[37,8,128]{2,1,0:T(8,128)S(1)}, f32[37,8,128]{2,1,0:T(8,128)S(1)}, u32[]{:S(2)}, u32[]{:S(2)}) collective-permute-start(f32[37,8,128]{2,1,0:T(8,128)S(1)} %collective-permute-done.partner_ref), channel_id=1, source_target_pairs={{0,16},{16,32},{32,48},{48,64},{64,80},{80,96},{96,112},{112,128},... | collective-permute-start | bytes 454664 | tf_op jit(solution)/shard_map/ppermute | solution.py:452

commit v3 on v1

--- a/solution.py
+++ b/solution.py
@@ -169,10 +169,12 @@
             ref[ROWS * RADIX, ROWS + r : ROWS + r + 1, :] = jnp.full(
                 (1, LANES), mask_ref[r].astype(jnp.float32), jnp.float32
             )
-    for copy in copies[2:]:
-        copy.wait()
-    for ref, level in ((mine_ref, half), (other_ref, 1 - half)):
-        for f in range(8):
+    copies[2].wait()
+    copies[4].wait()
+    for f in range(8):
+        if f == 3:
+            copies[3].wait()
+        for ref, level in ((mine_ref, half), (other_ref, 1 - half)):
             for r in range(ROWS):
                 if f < 2:
                     row = winds_ref[f, level, r : r + 1, :]

time: 61.4 us -> 61.3 us (level)
  no operation moved by 1% of the time
where the time goes in v3:
time: 61.3 us; the launch traced here: 61 us
  blocking collectives  36.5 us (60%)
  starting transfers between devices  11.8 us (19%)
  Pallas kernels  6.72 us (11%)
  waiting for transfers between devices  5.27 us (9%)
  between operations  0.7 us (1%)
    all_to_all x1, blocking collectives, shards(): lax.all_to_all(send, ('half', 'lev'), split_axis=0, concat_axis=0, tiled=...  21.3 us
    all_to_all x1, blocking collectives, shards(): got = lax.all_to_all(send, 'lev', split_axis=0, concat_axis=0, tiled=True)  15.2 us
    ppermute x1, starting transfers between devices, shards(): near = lax.ppermute(mine, bands, ups + downs)  5.64 us
    ppermute x1, waiting for transfers between devices, shards(): far = lax.ppermute(partner, bands, ups + downs)  4.31 us
    ppermute x1, starting transfers between devices, shards(): partner = lax.ppermute(other, bands, [(i, i ^ 1) for i in range(2 * pairs)])  4.28 us
    pallas_call x1, Pallas kernels, shards(): pl.pallas_call(early_kernel, out_shape=[pltpu.VMEM((2 * ROWS, 8, LON), jn...  1.99 us
    ppermute x1, starting transfers between devices, shards(): far = lax.ppermute(partner, bands, ups + downs)  1.92 us
    pallas_call x1, Pallas kernels, shards(): pl.pallas_call(late_kernel, out_shape=shape(16, 9, 4, LANES), in_specs=[V...  1.72 us
  transfers between devices with their start and end apart: 3, of which 2 were waited for; matrix products, arithmetic and copies ran while one was open for 0% of the time, Pallas kernels for 3%

profile of v3, /device:TPU:6, one launch (start us, length us, event | category | flops | bytes accessed | tf_op | source)
XLA Modules:
  0.0 61.0 jit_solution(10982977176777673694)
XLA Ops:
  0.6 0.0 copy-start
  0.6 0.0 copy-start.1
  0.7 0.0 copy-start.2
  0.7 1.2 %shard_map.103 = (f32[37,8,128]{2,1,0:T(8,128)S(1)}, f32[37,8,128]{2,1,0:T(8,128)S(1)}) custom-call(s32[4]{0:T(128)} %mask_hbm.1, s32[4]{0:T(128)} %cutoff_hbm.1, f32[2,2,4,1152]{3,2,1,0:T(4,128)} %winds_hbm.1, f32[5,2,4,1152]{3,2,1,0:T(4,128)} %fields_hbm.1, f32[2,4,1152]{2,1,0:T(4,128)} %thick_hbm.1), custom_call_target="tpu_custom_call" | custom-call | tf_op jit(solution)/shard_map/pallas_call | solution.py:435
  1.8 4.3 %collective-permute-start = (f32[37,8,128]{2,1,0:T(8,128)S(1)}, f32[37,8,128]{2,1,0:T(8,128)S(1)}, u32[]{:S(2)}, u32[]{:S(2)}) collective-permute-start(f32[37,8,128]{2,1,0:T(8,128)S(1)} %get-tuple-element.12), channel_id=1, source_target_pairs={{0,8},{8,0},{16,24},{24,16},{32,40},{40,32},{48,56},{56,48},{64,72... | collective-permute-start | bytes 454664 | tf_op jit(solution)/shard_map/ppermute | solution.py:451
  6.1 5.6 %collective-permute-start.2 = (f32[37,8,128]{2,1,0:T(8,128)S(1)}, f32[37,8,128]{2,1,0:T(8,128)S(1)}, u32[]{:S(2)}, u32[]{:S(2)}) collective-permute-start(f32[37,8,128]{2,1,0:T(8,128)S(1)} %get-tuple-element.11.mine_ref), channel_id=1, source_target_pairs={{8,24},{24,40},{40,56},{56,72},{72,88},{88,104},{104,120},{120,136... | collective-permute-start | bytes 454664 | tf_op jit(solution)/shard_map/ppermute | solution.py:450
  11.8 0.0 collective-permute-done.partner_ref
  11.8 1.9 %collective-permute-start.1 = (f32[37,8,128]{2,1,0:T(8,128)S(1)}, f32[37,8,128]{2,1,0:T(8,128)S(1)}, u32[]{:S(2)}, u32[]{:S(2)}) collective-permute-start(f32[37,8,128]{2,1,0:T(8,128)S(1)} %collective-permute-done.partner_ref), channel_id=1, source_target_pairs={{0,16},{16,32},{32,48},{48,64},{64,80},{80,96},{96,112},{112,128},... | collective-permute-start | bytes 454664 | tf_op jit(solution)/shard_map/ppermute | solution.py:454
  13.7 1.0 %collective-permute-done.2.near_ref = f32[37,8,128]{2,1,0:T(8,128)S(1)} collective-permute-done((f32[37,8,128]{2,1,0:T(8,128)S(1)}, f32[37,8,128]{2,1,0:T(8,128)S(1)}, u32[]{:S(2)}, u32[]{:S(2)}) %collective-permute-start.2) | collective-permute-done | bytes 151584 | tf_op jit(solution)/shard_map/ppermute | solution.py:450
  14.7 0.0 copy-done
  14.7 0.0 copy-done.1
  14.7 0.0 copy-done.2
  14.7 2.0 %shard_map.104 = (f32[8,8,1152]{2,1,0:T(8,128)S(1)}, f32[8,9,4,128]{3,2,1,0:T(4,128)S(1)}) custom-call(f32[37,8,128]{2,1,0:T(8,128)S(1)} %get-tuple-element.11.mine_ref, f32[37,8,128]{2,1,0:T(8,128)S(1)} %collective-permute-done.partner_ref, f32[37,8,128]{2,1,0:T(8,128)S(1)} %collective-permute-done.2.near_ref, f32[4,8,128]{2,1,0:T(8,128)S(1)} %copy-done.2, ...), custom_call_target="tpu_custom_call" | custom-call | bytes 3000000 | tf_op jit(solution)/shard_map/pallas_call | solution.py:459
  16.7 4.3 %collective-permute-done.1.far_ref = f32[37,8,128]{2,1,0:T(8,128)S(1)} collective-permute-done((f32[37,8,128]{2,1,0:T(8,128)S(1)}, f32[37,8,128]{2,1,0:T(8,128)S(1)}, u32[]{:S(2)}, u32[]{:S(2)}) %collective-permute-start.1) | collective-permute-done | bytes 151584 | tf_op jit(solution)/shard_map/ppermute | solution.py:454
  21.0 1.7 %shard_map.105 = f32[16,9,4,128]{3,2,1,0:T(4,128)S(1)} custom-call(f32[37,8,128]{2,1,0:T(8,128)S(1)} %get-tuple-element.11.mine_ref, f32[37,8,128]{2,1,0:T(8,128)S(1)} %collective-permute-done.1.far_ref, f32[8,8,1152]{2,1,0:T(8,128)S(1)} %get-tuple-element.13.early_ref, f32[8,9,4,128]{3,2,1,0:T(4,128)S(1)} %get-tuple-element.14.band_ref, ...), custom_call_target="tpu_custom_call" | custom-call | tf_op jit(solution)/shard_map/pallas_call | solution.py:473
  22.7 21.3 %all_to_all.10.got_ref = f32[16,9,4,128]{3,2,1,0:T(4,128)S(1)} all-to-all(f32[16,9,4,128]{3,2,1,0:T(4,128)S(1)} %shard_map.105), channel_id=1, replica_groups=mesh['pair'=32,'half'=2,'lev'=8] {'half','lev'}, dimensions={0} | all-to-all | bytes 589824 | tf_op jit(solution)/shard_map/all_to_all | solution.py:484
  44.0 0.9 %shard_map.106 = (f32[8,16,4,128]{3,2,1,0:T(4,128)S(1)}, f32[4,144]{1,0:T(4,128)}) custom-call(f32[16,9,4,128]{3,2,1,0:T(4,128)S(1)} %all_to_all.10.got_ref), custom_call_target="tpu_custom_call" | custom-call | tf_op jit(solution)/shard_map/pallas_call | solution.py:485
  44.9 15.2 %all_to_all.11.got_ref = f32[8,16,4,128]{3,2,1,0:T(4,128)S(1)} all-to-all(f32[8,16,4,128]{3,2,1,0:T(4,128)S(1)} %get-tuple-element.15), channel_id=1, replica_groups=mesh['pair'=32,'half'=2,'lev'=8] {'lev'}, dimensions={0} | all-to-all | bytes 524288 | tf_op jit(solution)/shard_map/all_to_all | solution.py:493
  60.1 0.9 %shard_map.107 = (f32[2,2,4,1152]{3,2,1,0:T(4,128)}, f32[5,2,4,1152]{3,2,1,0:T(4,128)}) custom-call(f32[8,16,4,128]{3,2,1,0:T(4,128)S(1)} %all_to_all.11.got_ref), custom_call_target="tpu_custom_call" | custom-call | tf_op jit(solution)/shard_map/pallas_call | solution.py:494
Async XLA Ops:
  0.6 14.0 %copy-start = (bf16[256,256]{1,0:T(8,128)(2,1)S(1)}, bf16[256,256]{1,0:T(8,128)(2,1)}, u32[]{:S(2)}) copy-start(bf16[256,256]{1,0:T(8,128)(2,1)} %constant.7.clone.high_ref) | copy-start | bytes 393220
  0.6 14.0 %copy-start.1 = (bf16[256,256]{1,0:T(8,128)(2,1)S(1)}, bf16[256,256]{1,0:T(8,128)(2,1)}, u32[]{:S(2)}) copy-start(bf16[256,256]{1,0:T(8,128)(2,1)} %constant.8.clone.low_ref) | copy-start | bytes 393220
  0.7 14.0 %copy-start.2 = (f32[4,8,128]{2,1,0:T(8,128)S(1)}, f32[4,8,128]{2,1,0:T(8,128)}, u32[]{:S(2)}) copy-start(f32[4,8,128]{2,1,0:T(8,128)} %constant.6.clone.table_ref) | copy-start | bytes 49156
  1.8 9.9 %collective-permute-start = (f32[37,8,128]{2,1,0:T(8,128)S(1)}, f32[37,8,128]{2,1,0:T(8,128)S(1)}, u32[]{:S(2)}, u32[]{:S(2)}) collective-permute-start(f32[37,8,128]{2,1,0:T(8,128)S(1)} %get-tuple-element.12), channel_id=1, source_target_pairs={{0,8},{8,0},{16,24},{24,16},{32,40},{40,32},{48,56},{56,48},{64,72... | collective-permute-start | bytes 454664 | tf_op jit(solution)/shard_map/ppermute | solution.py:451
  6.1 8.5 %collective-permute-start.2 = (f32[37,8,128]{2,1,0:T(8,128)S(1)}, f32[37,8,128]{2,1,0:T(8,128)S(1)}, u32[]{:S(2)}, u32[]{:S(2)}) collective-permute-start(f32[37,8,128]{2,1,0:T(8,128)S(1)} %get-tuple-element.11.mine_ref), channel_id=1, source_target_pairs={{8,24},{24,40},{40,56},{56,72},{72,88},{88,104},{104,120},{120,136... | collective-permute-start | bytes 454664 | tf_op jit(solution)/shard_map/ppermute | solution.py:450
  11.8 9.2 %collective-permute-start.1 = (f32[37,8,128]{2,1,0:T(8,128)S(1)}, f32[37,8,128]{2,1,0:T(8,128)S(1)}, u32[]{:S(2)}, u32[]{:S(2)}) collective-permute-start(f32[37,8,128]{2,1,0:T(8,128)S(1)} %collective-permute-done.partner_ref), channel_id=1, source_target_pairs={{0,16},{16,32},{32,48},{48,64},{64,80},{80,96},{96,112},{112,128},... | collective-permute-start | bytes 454664 | tf_op jit(solution)/shard_map/ppermute | solution.py:454
